TPU v7x, 1024 devices: a whole 4x8x16 slice. The times are simulated.
1024 devices in a mesh: group: 32 (over z, core), mp: 32 (over x, y).
Axes of the slice: x: 4, y: 8, z: 16, core: 2. Of those that a mesh axis runs over, the one named last changes fastest.
Arguments:
- base_rows: bfloat16 [16384, 16384], P('group', 'mp'), may hold values from -6 to 6
- cotangent: bfloat16 [16384, 16384], P('group', 'mp'), may hold values from -6 to 6
- in_panels: bfloat16 [32, 32, 512, 256], P(None, 'mp', 'group'), may hold values from -0.046875 to 0.046875
- out_panels: bfloat16 [32, 32, 512, 256], P(None, 'mp', 'group'), may hold values from -0.375 to 0.375
- gating_weight_matrix: bfloat16 [16384, 32], P('mp'), may hold values from -0.046875 to 0.046875
- cross_bias: float32 [16384], P('mp'), may hold values from -3 to 3
- dev_experts: int32 [32, 2], replicated, may hold values from 0 to 31, as said below
- block_slot: int32 [128], P('group'), may hold values from 0 to 1
- live_blocks: int32 [32], P('group'), may hold values from 1 to 4, as said below
Outputs:
- d_input: bfloat16 [16384, 16384], P('group', 'mp')
- d_in_panels: bfloat16 [32, 32, 512, 256], P(None, 'mp', 'group')
- d_out_panels: bfloat16 [32, 32, 512, 256], P(None, 'mp', 'group')
Inputs may be any that keep to these rules, and one draw needn't show every extreme that they name: `dev_experts`: each row names 2 different experts. `live_blocks`: A group's live blocks are its first ones; the others contribute nothing.
All inputs are finite; a program needn't handle non-finite values.
Results may differ from a plain program's by a relative error of at most 0.0057.
Values may be sent and summed in bfloat16 or wider, within the bound.
A program may use at most 32 MiB of HBM per device.

v0:
```python
import jax
import jax.numpy as jnp
from jax import lax
from jax.sharding import PartitionSpec as P


def per_device(
    base_rows,
    cotangent,
    in_panels,
    out_panels,
    gating_weight_matrix,
    cross_bias,
    dev_experts,
    block_slot,
    live_blocks,
):
    groups = lax.axis_size("group")
    slot_count = dev_experts.shape[1]
    experts = in_panels.shape[0]
    piece_rows = in_panels.shape[2]
    rank_size = in_panels.shape[3]
    slice_width = base_rows.shape[1]
    blocks = block_slot.shape[0]
    block_rows = base_rows.shape[0] // blocks
    group_id = lax.axis_index("group")
    my_experts = lax.dynamic_index_in_dim(dev_experts, group_id, 0, keepdims=False)
    block_expert = jnp.take(my_experts, block_slot)
    live_mask = (jnp.arange(blocks, dtype=jnp.int32) < live_blocks[0]).astype(jnp.float32)[
        :, None, None
    ]
    in_store = in_panels.reshape(experts, piece_rows, rank_size)
    out_store = out_panels.reshape(experts, piece_rows, rank_size)
    wanted = jnp.transpose(dev_experts)
    in_send = jnp.take(in_store, wanted, axis=0)
    out_send = jnp.take(out_store, wanted, axis=0)
    in_recv, out_recv = (
        lax.all_to_all(in_send, "group", split_axis=1, concat_axis=1, tiled=True),
        lax.all_to_all(out_send, "group", split_axis=1, concat_axis=1, tiled=True),
    )
    input_block_tile = jnp.take(
        in_recv.reshape(slot_count, slice_width, rank_size), block_slot, axis=0
    )
    output_block_tile = jnp.take(
        out_recv.reshape(slot_count, slice_width, rank_size), block_slot, axis=0
    )
    half_of_rows = base_rows.reshape(blocks, block_rows, slice_width)
    cot_half = cotangent.reshape(blocks, block_rows, slice_width)
    rows_full = half_of_rows.astype(jnp.float32)
    cot_full = cot_half.astype(jnp.float32)
    rank_portion = jnp.einsum(
        "vxh,vhg->vxg", half_of_rows, input_block_tile, preferred_element_type=jnp.float32
    )
    gating_scores = jnp.einsum(
        "mus,sq->muq", half_of_rows, gating_weight_matrix, preferred_element_type=jnp.float32
    )
    expert_hot = (block_expert[:, None] == jnp.arange(experts, dtype=jnp.int32)[None, :]).astype(
        jnp.float32
    )
    logit_part = jnp.sum(gating_scores * expert_hot[:, None, :], axis=2)
    rank_in, logit = lax.psum((rank_portion, logit_part), "mp")
    tanh_full = jnp.tanh(rank_in)
    hyperbolic_half = tanh_full.astype(jnp.bfloat16)
    cross = (
        jnp.einsum(
            "pvw,plw->pvl", hyperbolic_half, output_block_tile, preferred_element_type=jnp.float32
        )
        + cross_bias[None, None, :]
    )
    gate_prob = jax.nn.sigmoid(logit)[:, :, None]
    scaled = live_mask * gate_prob
    gated_row_half = (scaled * rows_full * cot_full).astype(jnp.bfloat16)

    def slot_sums(leftward_rows, rightward_rows):
        per_block = jnp.einsum(
            "enw,env->ewv", leftward_rows, rightward_rows, preferred_element_type=jnp.float32
        )
        summed = []
        for slot_id in range(slot_count):
            slot_mask = (block_slot == slot_id).astype(jnp.float32)[:, None, None]
            summed.append(jnp.sum(per_block * slot_mask, axis=0))
        return jnp.stack(summed, axis=0).reshape(slot_count, groups, piece_rows, rank_size)

    def owner_sums(received):
        total = jnp.zeros((experts, piece_rows, rank_size), jnp.float32).at[wanted].add(received)
        return total.astype(jnp.bfloat16).reshape(experts, 1, piece_rows, rank_size)

    back_part = jnp.einsum(
        "vxh,vhg->vxg", gated_row_half, output_block_tile, preferred_element_type=jnp.float32
    )
    gate_part = jnp.sum(rows_full * cross * cot_full, axis=2)
    back_rank, gate_sum = lax.psum((back_part, gate_part), "mp")
    gate_back = scaled * (1.0 - gate_prob) * gate_sum[:, :, None]
    rank_gradient = (back_rank * (1.0 - tanh_full * tanh_full)).astype(jnp.bfloat16)
    gate_cols = jnp.transpose(
        jnp.take(gating_weight_matrix, block_expert, axis=1).astype(jnp.float32)
    )
    d_rows = cot_full * (1.0 + scaled * cross)
    d_rows = d_rows + jnp.einsum(
        "pvw,plw->pvl", rank_gradient, input_block_tile, preferred_element_type=jnp.float32
    )
    d_rows = d_rows + gate_back * gate_cols[:, None, :]
    d_input = d_rows.astype(jnp.bfloat16).reshape(blocks * block_rows, slice_width)
    out_grads, in_grads = (
        lax.all_to_all(
            slot_sums(gated_row_half, hyperbolic_half),
            "group",
            split_axis=1,
            concat_axis=1,
            tiled=True,
        ),
        lax.all_to_all(
            slot_sums(half_of_rows, rank_gradient), "group", split_axis=1, concat_axis=1, tiled=True
        ),
    )
    return (d_input, owner_sums(in_grads), owner_sums(out_grads))


def solution(mesh):
    placed = (
        P("group", "mp"),
        P("group", "mp"),
        P(None, "mp", "group", None),
        P(None, "mp", "group", None),
        P("mp", None),
        P("mp"),
        P(),
        P("group"),
        P("group"),
    )
    return jax.shard_map(
        per_device,
        mesh=mesh,
        in_specs=placed,
        out_specs=(P("group", "mp"), P(None, "mp", "group", None), P(None, "mp", "group", None)),
        check_vma=False,
    )
```

profile of v0, /device:TPU:1, one launch (start us, length us, event | category | flops | bytes accessed | tf_op | source)
XLA Modules:
  0.0 606.5 jit_solution(5693942134328151963)
XLA Ops:
  7.2 0.7 compare_select_fusion
  10.1 0.9 copy.34
  11.0 20.4 %all-to-all-start = ((bf16[2,32,16,256]{3,2,0,1:T(8,128)(2,1)}), bf16[2,32,16,256]{3,2,0,1:T(8,128)(2,1)S(1)}, u32[]{:S(2)}, u32[]{:S(2)}) async-start(bf16[2,32,16,256]{3,2,0,1:T(8,128)(2,1)} %copy.34), calls=%async_computation | async-start | bytes 1048576 | tf_op jit(solution)/shard_map/all_to_all | solution.py:38
  31.4 0.9 copy.37
  32.3 32.6 %all-to-all-done = bf16[2,32,16,256]{3,2,0,1:T(8,128)(2,1)S(1)} async-done(((bf16[2,32,16,256]{3,2,0,1:T(8,128)(2,1)}), bf16[2,32,16,256]{3,2,0,1:T(8,128)(2,1)S(1)}, u32[]{:S(2)}, u32[]{:S(2)}) %all-to-all-start) | async-done | bytes 524320 | tf_op jit(solution)/shard_map/all_to_all | solution.py:38
  64.9 4.0 all-to-all-start.1
  71.0 1.4 convolution_bitcast_fusion
  73.4 29.1 %all-to-all-done.1 = bf16[2,32,16,256]{3,2,0,1:T(8,128)(2,1)S(1)} async-done(((bf16[2,32,16,256]{3,2,0,1:T(8,128)(2,1)}), bf16[2,32,16,256]{3,2,0,1:T(8,128)(2,1)S(1)}, u32[]{:S(2)}, u32[]{:S(2)}) %all-to-all-start.1) | async-done | bytes 524320 | tf_op jit(solution)/shard_map/all_to_all | solution.py:39
  103.2 146.2 %all-reduce.4.cloned.1.call-done = f32[4,128,256]{1,2,0:T(8,128)} async-done(((f32[4,128,256]{1,2,0:T(8,128)}), f32[4,128,256]{1,2,0:T(8,128)}) %all-reduce.4.cloned.1.call-update) | async-done | bytes 524304 | tf_op jit(solution)/shard_map/psum | solution.py:61
  249.4 2.7 fusion.4
  252.1 58.5 %all-reduce = (f32[4,128]{1,0:T(4,128)S(1)}, f32[4,128]{1,0:T(4,128)S(1)}) all-reduce(f32[4,128]{1,0:T(4,128)S(1)} %fusion.2, f32[4,128]{1,0:T(4,128)S(1)} %get-tuple-element.20), channel_id=1, replica_groups=mesh['group'=32,'mp'=32] {'mp'}, use_global_device_ids=true, to_apply=%region_1.2 | all-reduce | flops 1024 | bytes 8192 | tf_op jit(solution)/shard_map/psum | solution.py:61
  310.6 0.7 multiply_reduce_fusion.1
  311.4 1.1 pad_maximum_fusion.1
  312.4 32.2 %all-to-all-start.3 = ((f32[2,32,16,256]{3,2,0,1:T(8,128)}), f32[2,32,16,256]{3,2,0,1:T(8,128)S(1)}, u32[]{:S(2)}, u32[]{:S(2)}) async-start(f32[2,32,16,256]{3,2,0,1:T(8,128)} %pad_maximum_fusion.1), calls=%async_computation.3 | async-start | bytes 2097152 | tf_op jit(solution)/shard_map/all_to_all | solution.py:105
  344.7 2.6 fusion.5
  347.3 170.9 %all-reduce.6.cloned.1.call-done = f32[4,128,256]{1,2,0:T(8,128)} async-done(((f32[4,128,256]{1,2,0:T(8,128)}), f32[4,128,256]{1,2,0:T(8,128)}) %all-reduce.6.cloned.1.call-update) | async-done | bytes 524304 | tf_op jit(solution)/shard_map/psum | solution.py:92
  518.3 1.2 multiply_convert_fusion
  520.6 1.1 copy.44
  521.7 18.2 %all-to-all-start.2 = ((f32[2,32,16,256]{3,2,0,1:T(8,128)}), f32[2,32,16,256]{3,2,0,1:T(8,128)S(1)}, u32[]{:S(2)}, u32[]{:S(2)}) async-start(f32[2,32,16,256]{3,2,0,1:T(8,128)} %copy.44), calls=%async_computation.2 | async-start | bytes 2097152 | tf_op jit(solution)/shard_map/all_to_all | solution.py:112
  541.2 2.8 fusion.1
  544.1 3.1 scatter_fusion.1
  547.3 0.7 convert_bitcast_fusion
  548.0 47.7 %all-to-all-done.2 = f32[2,32,16,256]{3,2,0,1:T(8,128)S(1)} async-done(((f32[2,32,16,256]{3,2,0,1:T(8,128)}), f32[2,32,16,256]{3,2,0,1:T(8,128)S(1)}, u32[]{:S(2)}, u32[]{:S(2)}) %all-to-all-start.2) | async-done | bytes 1048608 | tf_op jit(solution)/shard_map/all_to_all | solution.py:112
  595.8 3.1 scatter_fusion
  (61 shorter events, 8.6 us)
Async XLA Ops:
  7.2 1.5 copy-start
  7.2 2.1 copy-start.6
  11.0 53.9 %all-to-all-start = ((bf16[2,32,16,256]{3,2,0,1:T(8,128)(2,1)}), bf16[2,32,16,256]{3,2,0,1:T(8,128)(2,1)S(1)}, u32[]{:S(2)}, u32[]{:S(2)}) async-start(bf16[2,32,16,256]{3,2,0,1:T(8,128)(2,1)} %copy.34), calls=%async_computation | async-start | bytes 1048576 | tf_op jit(solution)/shard_map/all_to_all | solution.py:38
  31.4 37.6 %copy-start.9 = (s32[32,2]{0,1:T(2,128)S(1)}, s32[32,2]{0,1:T(2,128)}, u32[]{:S(2)}) copy-start(s32[32,2]{0,1:T(2,128)} %param.19) | copy-start | bytes 772
  31.4 37.8 %copy-start.11 = (s32[4]{0:T(128)S(1)}, s32[4]{0:T(128)}, u32[]{:S(2)}) copy-start(s32[4]{0:T(128)} %param.20) | copy-start | bytes 52
  64.9 37.6 %all-to-all-start.1 = ((bf16[2,32,16,256]{3,2,0,1:T(8,128)(2,1)}), bf16[2,32,16,256]{3,2,0,1:T(8,128)(2,1)S(1)}, u32[]{:S(2)}, u32[]{:S(2)}) async-start(bf16[2,32,16,256]{3,2,0,1:T(8,128)(2,1)} %copy.37), calls=%async_computation.1 | async-start | bytes 1048576 | tf_op jit(solution)/shard_map/all_to_all | solution.py:39
  68.9 180.4 %all-reduce.4.cloned.1.call-start = ((), (), s32[]{:S(2)}) async-start(), calls=%async_computation.4 | async-start | bytes 1048576 | tf_op jit(solution)/shard_map/psum | solution.py:61
  69.9 1.0 copy-start.2
  70.5 32.0 %copy-start.5 = (bf16[4,512,256]{2,1,0:T(8,128)(2,1)}, bf16[4,512,256]{2,1,0:T(8,128)(2,1)S(1)}, u32[]{:S(2)}) copy-start(bf16[4,512,256]{2,1,0:T(8,128)(2,1)S(1)} %gather_fusion.3) | copy-start | bytes 3145732
  71.0 2.2 copy-start.1
  102.5 146.8 %copy-start.7 = (bf16[512,512]{1,0:T(8,128)(2,1)S(1)}, bf16[512,512]{1,0:T(8,128)(2,1)}, u32[]{:S(2)}) copy-start(bf16[512,512]{1,0:T(8,128)(2,1)} %param.14) | copy-start | bytes 1572868
  102.5 146.8 %copy-start.10 = (f32[512]{0:T(512)S(1)}, f32[512]{0:T(512)}, u32[]{:S(2)}) copy-start(f32[512]{0:T(512)} %param.18) | copy-start | bytes 6148
  249.4 61.3 %copy-start.3 = (f32[4,128,256]{1,2,0:T(8,128)S(1)}, f32[4,128,256]{1,2,0:T(8,128)}, u32[]{:S(2)}) copy-start(f32[4,128,256]{1,2,0:T(8,128)} %all-reduce.4.cloned.1.call-done) | copy-start | bytes 1572868
  312.4 209.3 %all-to-all-start.3 = ((f32[2,32,16,256]{3,2,0,1:T(8,128)}), f32[2,32,16,256]{3,2,0,1:T(8,128)S(1)}, u32[]{:S(2)}, u32[]{:S(2)}) async-start(f32[2,32,16,256]{3,2,0,1:T(8,128)} %pad_maximum_fusion.1), calls=%async_computation.3 | async-start | bytes 2097152 | tf_op jit(solution)/shard_map/all_to_all | solution.py:105
  344.7 173.6 %all-reduce.6.cloned.1.call-start = ((), (), s32[]{:S(2)}) async-start(), calls=%async_computation.5 | async-start | bytes 1048576 | tf_op jit(solution)/shard_map/psum | solution.py:92
  519.4 0.7 copy-start.8
  521.7 74.0 %all-to-all-start.2 = ((f32[2,32,16,256]{3,2,0,1:T(8,128)}), f32[2,32,16,256]{3,2,0,1:T(8,128)S(1)}, u32[]{:S(2)}, u32[]{:S(2)}) async-start(f32[2,32,16,256]{3,2,0,1:T(8,128)} %copy.44), calls=%async_computation.2 | async-start | bytes 2097152 | tf_op jit(solution)/shard_map/all_to_all | solution.py:112
  539.9 1.2 copy-start.4
Sparse Core Ops, SparseCore 0:
  73.2 176.1 all-reduce.3
  349.8 168.3 all-reduce.5
where the time goes:
time: 607 us
  waiting for transfers between devices  426 us (70%)
  starting transfers between devices  75 us (12%)
  blocking collectives  58.5 us (10%)
  between operations  15 us (2%)
  other arithmetic  11.9 us (2%)
  matrix products  11.1 us (2%)
  local copies, waits for them, and re-layouts  8.61 us (1%)
    psum x1, waiting for transfers between devices, per_device(): back_rank, gate_sum = lax.psum((back_part, gate_part), 'mp')  171 us
    psum x1, waiting for transfers between devices, per_device(): rank_in, logit = lax.psum((rank_portion, logit_part), 'mp')  146 us
    psum x1, blocking collectives, per_device(): rank_in, logit = lax.psum((rank_portion, logit_part), 'mp')  58.5 us
    all_to_all x1, waiting for transfers between devices, per_device(): lax.all_to_all(slot_sums(half_of_rows, rank_gradient), 'group', split_axi...  47.7 us
    all_to_all x1, waiting for transfers between devices, per_device(): lax.all_to_all(in_send, 'group', split_axis=1, concat_axis=1, tiled=True)  32.6 us
    all_to_all x1, starting transfers between devices, per_device(): lax.all_to_all(slot_sums(gated_row_half, hyperbolic_half), 'group', split...  32.2 us
    all_to_all x1, waiting for transfers between devices, per_device(): lax.all_to_all(out_send, 'group', split_axis=1, concat_axis=1, tiled=True)  29.1 us
    all_to_all x1, starting transfers between devices, per_device(): lax.all_to_all(in_send, 'group', split_axis=1, concat_axis=1, tiled=True)  20.4 us
  transfers between devices with their start and end apart: 6, of which 5 were waited for; matrix products, arithmetic and copies ran while one was open for 3% of the time, Pallas kernels for 0%

commit v1 on v0

v1 whole, which is shorter than its diff:
```python
import functools

import jax
import jax.numpy as jnp
from jax import lax
from jax.experimental import pallas as pl
from jax.experimental.pallas import tpu as pltpu
from jax.sharding import PartitionSpec as P

F32 = jnp.float32
BF16 = jnp.bfloat16
NT = (((1,), (1,)), ((), ()))
TN = (((0,), (0,)), ((), ()))
LOGIT, VPANEL, UPANEL, RANK, TANH, DOUT, BACK, RGRAD, GSUM, DIN = range(10)


def kernel(
    groups,
    mps,
    dev_ref,
    slot_ref,
    live_ref,
    code_ref,
    x_ref,
    g_ref,
    vin_ref,
    uin_ref,
    gate_ref,
    bias_ref,
    dx_ref,
    din_ref,
    dout_ref,
    vstage,
    ustage,
    vrecv,
    urecv,
    lsend,
    lrecv,
    rsend,
    rrecv,
    tanh_all,
    tanh_own,
    bsend,
    brecv,
    rgrad,
    qsend,
    qrecv,
    gated,
    dpart,
    osend,
    orecv,
    isend,
    irecv,
    send,
    recv,
):
    h = lax.axis_index("group")
    m = lax.axis_index("mp")
    experts, piece, rank = vin_ref.shape
    rows, width = x_ref.shape
    blocks = slot_ref.shape[0]
    block_rows = rows // blocks
    shard = rows // mps
    slots = dev_ref.shape[1]

    def offset(i, n):
        k = i // 2 + 1
        return (i % 2) * (n - 2 * k) + k

    def to_groups(which, src, dst):
        def step(i, carry):
            j = lax.rem(h + offset(i, groups), groups)
            pltpu.make_async_remote_copy(
                src_ref=src(j),
                dst_ref=dst,
                send_sem=send.at[which],
                recv_sem=recv.at[which],
                device_id={"group": j},
                device_id_type=pl.DeviceIdType.MESH,
            ).start()
            return carry

        lax.fori_loop(0, groups - 1, step, 0)

    def to_mps(which, src, dst):
        def step(i, carry):
            j = lax.rem(m + offset(i, mps), mps)
            pltpu.make_async_remote_copy(
                src_ref=src(j),
                dst_ref=dst,
                send_sem=send.at[which],
                recv_sem=recv.at[which],
                device_id={"mp": j},
                device_id_type=pl.DeviceIdType.MESH,
            ).start()
            return carry

        lax.fori_loop(0, mps - 1, step, 0)

    def drain(ref, sem):
        pltpu.make_async_copy(ref, ref, sem).wait()

    def block(b):
        return pl.ds(b * block_rows, block_rows)

    def part(j, size):
        return pl.ds(pl.multiple_of(j * size, size), size)

    def column(row):
        square = jnp.transpose(jnp.broadcast_to(row, (block_rows, block_rows)))
        return jnp.concatenate([square] * (width // block_rows), axis=1)

    barrier = pltpu.get_barrier_semaphore()

    for axis, me, n in (("group", h, groups), ("mp", m, mps)):

        def greet(i, carry, axis=axis, me=me, n=n):
            pl.semaphore_signal(
                barrier,
                inc=1,
                device_id={axis: lax.rem(me + i, n)},
                device_id_type=pl.DeviceIdType.MESH,
            )
            return carry

        lax.fori_loop(1, n, greet, 0)

    def stage(j, carry):
        for s in range(slots):
            e = dev_ref[j, s]
            vstage[j, s] = vin_ref[e]
            ustage[j, s] = uin_ref[e]
        return carry

    lax.fori_loop(0, groups, stage, 0)
    for s in range(slots):
        vrecv[s, part(h, piece), :] = vstage[h, s]
        urecv[s, part(h, piece), :] = ustage[h, s]

    slot_of = [slot_ref[b] for b in range(blocks)]
    gate_row = [gate_ref[dev_ref[h, slot_of[b]]] for b in range(blocks)]
    alive = [(live_ref[0] > b).astype(F32) for b in range(blocks)]
    which_row = lax.broadcasted_iota(jnp.int32, (8, block_rows), 0)
    logits = jnp.zeros((8, block_rows), F32)
    live_rows = jnp.zeros((8, block_rows), F32)
    for b in range(blocks):
        wide = jnp.broadcast_to(gate_row[b], (8, width)).astype(BF16)
        scores = lax.dot_general(wide, x_ref[block(b), :], NT, preferred_element_type=F32)
        logits = jnp.where(which_row == b, scores, logits)
        live_rows = jnp.where(which_row == b, alive[b], live_rows)
    lsend[...] = logits
    lrecv[m] = logits

    pl.semaphore_wait(barrier, groups + mps - 2)

    to_groups(VPANEL, lambda j: vstage.at[j], vrecv.at[:, part(h, piece), :])
    to_mps(LOGIT, lambda j: lsend, lrecv.at[m])
    drain(lrecv.at[pl.ds(0, mps - 1)], recv.at[LOGIT])
    prob = jax.nn.sigmoid(jnp.sum(lrecv[...], axis=0))
    scaled = live_rows * prob
    for b in range(blocks):
        gate = column(scaled[b : b + 1, :])
        gated[block(b), :] = (
            gate * x_ref[block(b), :].astype(F32) * g_ref[block(b), :].astype(F32)
        ).astype(BF16)

    drain(vrecv.at[:, pl.ds(0, width - piece), :], recv.at[VPANEL])
    to_groups(UPANEL, lambda j: ustage.at[j], urecv.at[:, part(h, piece), :])
    for b in range(blocks):
        rsend[block(b), :] = jnp.dot(
            x_ref[block(b), :], vrecv[slot_of[b]], preferred_element_type=F32
        ).astype(rsend.dtype)
    to_mps(RANK, lambda j: rsend.at[part(j, shard), :], rrecv.at[m])
    rrecv[m] = rsend[part(m, shard), :]
    drain(rrecv.at[pl.ds(0, mps - 1)], recv.at[RANK])
    tanh_full = jnp.tanh(jnp.sum(rrecv[...].astype(F32), axis=0))
    tanh_own[...] = tanh_full
    tanh_all[part(m, shard), :] = tanh_full.astype(BF16)
    mine = tanh_all.at[part(m, shard), :]
    to_mps(TANH, lambda j: mine, mine)
    drain(tanh_all.at[pl.ds(0, rows - shard), :], recv.at[TANH])

    def by_slot(value):
        parts = []
        for s in range(slots):
            held = [
                value[b * block_rows : (b + 1) * block_rows, :]
                * (slot_of[b] == s).astype(F32).astype(BF16)
                for b in range(blocks)
            ]
            parts.append(jnp.concatenate(held, axis=0))
        return parts

    for s, right in enumerate(by_slot(tanh_all[...])):
        osend[s] = lax.dot_general(gated[...], right, TN, preferred_element_type=F32).astype(
            osend.dtype
        )
    to_groups(DOUT, lambda j: osend.at[:, part(j, piece), :], orecv.at[h])
    orecv[h] = osend[:, part(h, piece), :]

    drain(urecv.at[:, pl.ds(0, width - piece), :], recv.at[UPANEL])
    for b in range(blocks):
        bsend[block(b), :] = jnp.dot(
            gated[block(b), :], urecv[slot_of[b]], preferred_element_type=F32
        ).astype(bsend.dtype)
    to_mps(BACK, lambda j: bsend.at[part(j, shard), :], brecv.at[m])
    brecv[m] = bsend[part(m, shard), :]

    sums = jnp.zeros((8, block_rows), F32)
    for b in range(blocks):
        cross = (
            lax.dot_general(
                tanh_all[block(b), :], urecv[slot_of[b]], NT, preferred_element_type=F32
            )
            + bias_ref[...]
        )
        gate = column(scaled[b : b + 1, :])
        full = g_ref[block(b), :].astype(F32)
        dpart[block(b), :] = full * (1.0 + gate * cross)
        product = x_ref[block(b), :].astype(F32) * cross * full
        folded = product[:, :block_rows]
        for c in range(1, width // block_rows):
            folded = folded + product[:, c * block_rows : (c + 1) * block_rows]
        row = jnp.sum(jnp.transpose(folded), axis=0, keepdims=True)
        sums = jnp.where(which_row == b, row, sums)
    qsend[...] = sums
    qrecv[m] = sums
    to_mps(GSUM, lambda j: qsend, qrecv.at[m])

    drain(brecv.at[pl.ds(0, mps - 1)], recv.at[BACK])
    back_rank = jnp.sum(brecv[...].astype(F32), axis=0)
    tanh_mine = tanh_own[...]
    rgrad[part(m, shard), :] = (back_rank * (1.0 - tanh_mine * tanh_mine)).astype(BF16)
    own = rgrad.at[part(m, shard), :]
    to_mps(RGRAD, lambda j: own, own)
    drain(rgrad.at[pl.ds(0, rows - shard), :], recv.at[RGRAD])
    for s, right in enumerate(by_slot(rgrad[...])):
        isend[s] = lax.dot_general(x_ref[...], right, TN, preferred_element_type=F32).astype(
            isend.dtype
        )
    to_groups(DIN, lambda j: isend.at[:, part(j, piece), :], irecv.at[h])
    irecv[h] = isend[:, part(h, piece), :]

    drain(qrecv.at[pl.ds(0, mps - 1)], recv.at[GSUM])
    gate_back = scaled * (1.0 - prob) * jnp.sum(qrecv[...], axis=0)
    for b in range(blocks):
        total = dpart[block(b), :] + lax.dot_general(
            rgrad[block(b), :], vrecv[slot_of[b]], NT, preferred_element_type=F32
        )
        total = total + column(gate_back[b : b + 1, :]) * gate_row[b]
        dx_ref[block(b), :] = total.astype(BF16)

    owners = (
        lax.broadcasted_iota(jnp.int32, (experts * piece, groups * slots * piece), 0)
        == code_ref[...]
    ).astype(F32).astype(BF16)

    def owner_sums(received, out):
        flat = received[...].reshape(groups * slots * piece, rank)
        total = jnp.dot(owners, flat, preferred_element_type=F32)
        out[...] = total.astype(BF16).reshape(experts, piece, rank)

    drain(orecv.at[pl.ds(0, groups - 1)], recv.at[DOUT])
    owner_sums(orecv, dout_ref)
    drain(irecv.at[pl.ds(0, groups - 1)], recv.at[DIN])
    owner_sums(irecv, din_ref)

    drain(vstage.at[pl.ds(0, groups - 1)], send.at[VPANEL])
    drain(ustage.at[pl.ds(0, groups - 1)], send.at[UPANEL])
    drain(orecv.at[pl.ds(0, groups - 1)], send.at[DOUT])
    drain(irecv.at[pl.ds(0, groups - 1)], send.at[DIN])
    drain(lrecv.at[pl.ds(0, mps - 1)], send.at[LOGIT])
    drain(qrecv.at[pl.ds(0, mps - 1)], send.at[GSUM])
    drain(rrecv.at[pl.ds(0, mps - 1)], send.at[RANK])
    drain(brecv.at[pl.ds(0, mps - 1)], send.at[BACK])
    drain(tanh_all.at[pl.ds(0, rows - shard), :], send.at[TANH])
    drain(rgrad.at[pl.ds(0, rows - shard), :], send.at[RGRAD])


def per_device(
    base_rows,
    cotangent,
    in_panels,
    out_panels,
    gating_weight_matrix,
    cross_bias,
    dev_experts,
    block_slot,
    live_blocks,
):
    groups = lax.axis_size("group")
    mps = lax.axis_size("mp")
    slots = dev_experts.shape[1]
    experts, _, piece, rank = in_panels.shape
    rows, width = base_rows.shape
    shard = rows // mps
    lanes = rows // block_slot.shape[0]
    gates = jnp.transpose(gating_weight_matrix).astype(F32).reshape(experts, 1, width)
    code = (
        dev_experts.reshape(groups * slots, 1) * piece + jnp.arange(piece, dtype=jnp.int32)[None, :]
    ).reshape(1, groups * slots * piece)
    vmem = pl.BlockSpec(memory_space=pltpu.VMEM)
    smem = pl.BlockSpec(memory_space=pltpu.SMEM)
    dx, din, dout = pl.pallas_call(
        functools.partial(kernel, groups, mps),
        out_shape=(
            jax.ShapeDtypeStruct((rows, width), BF16),
            jax.ShapeDtypeStruct((experts, piece, rank), BF16),
            jax.ShapeDtypeStruct((experts, piece, rank), BF16),
        ),
        in_specs=[smem] * 3 + [vmem] * 7,
        out_specs=(vmem, vmem, vmem),
        scratch_shapes=[
            pltpu.VMEM((groups, slots, piece, rank), BF16),
            pltpu.VMEM((groups, slots, piece, rank), BF16),
            pltpu.VMEM((slots, width, rank), BF16),
            pltpu.VMEM((slots, width, rank), BF16),
            pltpu.VMEM((8, lanes), F32),
            pltpu.VMEM((mps, 8, lanes), F32),
            pltpu.VMEM((rows, rank), BF16),
            pltpu.VMEM((mps, shard, rank), BF16),
            pltpu.VMEM((rows, rank), BF16),
            pltpu.VMEM((shard, rank), F32),
            pltpu.VMEM((rows, rank), BF16),
            pltpu.VMEM((mps, shard, rank), BF16),
            pltpu.VMEM((rows, rank), BF16),
            pltpu.VMEM((8, lanes), F32),
            pltpu.VMEM((mps, 8, lanes), F32),
            pltpu.VMEM((rows, width), BF16),
            pltpu.VMEM((rows, width), F32),
            pltpu.VMEM((slots, width, rank), BF16),
            pltpu.VMEM((groups, slots, piece, rank), BF16),
            pltpu.VMEM((slots, width, rank), BF16),
            pltpu.VMEM((groups, slots, piece, rank), BF16),
            pltpu.SemaphoreType.DMA((10,)),
            pltpu.SemaphoreType.DMA((10,)),
        ],
        compiler_params=pltpu.CompilerParams(
            collective_id=0, has_side_effects=True, vmem_limit_bytes=40 * 1024 * 1024
        ),
    )(
        dev_experts,
        block_slot,
        live_blocks,
        code,
        base_rows,
        cotangent,
        in_panels.reshape(experts, piece, rank),
        out_panels.reshape(experts, piece, rank),
        gates,
        cross_bias.reshape(1, width),
    )
    return (
        dx,
        din.reshape(experts, 1, piece, rank),
        dout.reshape(experts, 1, piece, rank),
    )


def solution(mesh):
    placed = (
        P("group", "mp"),
        P("group", "mp"),
        P(None, "mp", "group", None),
        P(None, "mp", "group", None),
        P("mp", None),
        P("mp"),
        P(),
        P("group"),
        P("group"),
    )
    return jax.shard_map(
        per_device,
        mesh=mesh,
        in_specs=placed,
        out_specs=(P("group", "mp"), P(None, "mp", "group", None), P(None, "mp", "group", None)),
        check_vma=False,
    )
```

time: 607 us -> 137 us (0.23)
  waiting for transfers between devices: 426 us -> 0 us
  Pallas kernels: 0 us -> 127 us
  starting transfers between devices: 75 us -> 0 us
  blocking collectives: 58.5 us -> 0 us
  between operations: 15 us -> 1.37 us
  matrix products: 11.1 us -> 0 us
  other arithmetic: 11.9 us -> 1.53 us
    psum x2 -> x0, waiting for transfers between devices: 317 us -> none  [the longest x1 171 us: per_device(): back_rank, gate_sum = lax.psum((back_part, gate_part), 'mp')]
    pallas_call x0 -> x1, Pallas kernels: none -> 127 us  [per_device(): pl.pallas_call(functools.partial(kernel, groups, mps), out_shape=(jax.Sha...]
    all_to_all x4 -> x0, waiting for transfers between devices: 109 us -> none  [the longest x1 47.7 us: per_device(): lax.all_to_all(slot_sums(half_of_rows, rank_gradient), 'group', split_axi...]
    all_to_all x4 -> x0, starting transfers between devices: 74.9 us -> none  [the longest x1 32.2 us: per_device(): lax.all_to_all(slot_sums(gated_row_half, hyperbolic_half), 'group', split...]
    psum x1 -> x0, blocking collectives: 58.5 us -> none  [per_device(): rank_in, logit = lax.psum((rank_portion, logit_part), 'mp')]
    dot_general x7 -> x0, matrix products: 11.1 us -> none  [the longest x1 2.84 us: per_device(): jnp.einsum('pvw,plw->pvl', rank_gradient, input_block_tile, preferred_ele...]
    scatter-add x2 -> x0, other arithmetic: 6.27 us -> none  [owner_sums(): jnp.zeros((experts, piece_rows, rank_size), jnp.float32).at[wanted]]
  transfers between devices with their start and end apart: 6 -> 0, of which waited for: 5 -> 0; matrix products, arithmetic and copies ran while one was open for 3% -> 0% of each run, Pallas kernels for 0% -> 0%
where the time goes in v1:
time: 137 us; the launch traced here: 136 us
  Pallas kernels  127 us (93%)
  local copies, waits for them, and re-layouts  6.94 us (5%)
  other arithmetic  1.53 us (1%)
  between operations  1.37 us (1%)
    pallas_call x1, Pallas kernels, per_device(): pl.pallas_call(functools.partial(kernel, groups, mps), out_shape=(jax.Sha...  127 us
    unnamed x16, local copies, waits for them, and re-layouts  6.61 us

profile of v1, /device:TPU:1, one launch (start us, length us, event | category | flops | bytes accessed | tf_op | source)
XLA Modules:
  0.0 136.4 jit_solution(10123084532692987139)
XLA Ops:
  0.6 0.0 copy-start.2
  1.3 0.7 broadcast_multiply_fusion
  2.0 0.1 copy.16
  2.1 0.1 mul.16
  2.2 0.8 copy.17.dev_ref
  3.0 0.1 iota_add_fusion
  3.0 0.1 add.26.code_ref
  3.1 0.8 convert_bitcast_fusion
  3.9 0.0 copy-start.4
  3.9 0.0 copy-start.5
  4.0 0.0 copy-done.2
  4.0 0.6 copy-done.4
  4.6 0.0 copy-done.5
  4.6 0.0 copy-start
  4.6 1.0 copy-done
  5.6 0.0 copy-start.1
  5.6 1.0 copy-done.1
  6.7 0.0 copy-start.3
  6.7 0.9 copy-done.3
  7.6 126.5 %shard_map.112 = (bf16[512,512]{1,0:T(8,128)(2,1)S(1)}, bf16[32,16,256]{2,1,0:T(8,128)(2,1)S(1)}, bf16[32,16,256]{2,1,0:T(8,128)(2,1)S(1)}) custom-call(s32[32,2]{1,0:T(8,128)S(1)} %copy.17.dev_ref, s32[4]{0:T(128)S(1)} %copy-done.5, s32[1]{0:T(128)S(6)} %copy.23.live_ref, s32[1,1024]{1,0:T(1,128)S(1)} %add.26.code_ref, bf16[512,512]{1,0:T(8,128)(2,1)S(1)} %copy-done, ...), custom_call_target="tpu_custom_call" | custom-call | tf_op jit(solution)/shard_map/pallas_call | solution.py:304
  134.2 0.8 copy.24
  135.0 0.7 copy.25
  135.7 0.7 copy.26
  (1 shorter events, 0.0 us)
Async XLA Ops:
  0.6 3.3 %copy-start.2 = (bf16[32,1,16,256]{3,2,1,0:T(8,128)(2,1)S(1)}, bf16[32,1,16,256]{3,2,1,0:T(8,128)(2,1)}, u32[]{:S(2)}) copy-start(bf16[32,1,16,256]{3,2,1,0:T(8,128)(2,1)} %param.11) | copy-start | bytes 786436
  3.9 0.7 copy-start.4
  3.9 0.7 copy-start.5
  4.6 1.0 copy-start
  5.6 1.0 copy-start.1
  6.7 0.9 copy-start.3

commit v2 on v1

--- a/solution.py
+++ b/solution.py
@@ -12,6 +12,7 @@
 NT = (((1,), (1,)), ((), ()))
 TN = (((0,), (0,)), ((), ()))
 LOGIT, VPANEL, UPANEL, RANK, TANH, DOUT, BACK, RGRAD, GSUM, DIN = range(10)
+VIN, GATE, ROWS, COT, UIN, BIAS, DX_OUT, DIN_OUT, DOUT_OUT = range(9)
 
 
 def kernel(
@@ -20,16 +21,25 @@
     dev_ref,
     slot_ref,
     live_ref,
-    code_ref,
+    x_hbm,
+    g_hbm,
+    vin_hbm,
+    uin_hbm,
+    gate_hbm,
+    bias_hbm,
+    dx_hbm,
+    din_hbm,
+    dout_hbm,
+    dx_ref,
+    din_ref,
+    dout_ref,
     x_ref,
     g_ref,
     vin_ref,
     uin_ref,
     gate_ref,
     bias_ref,
-    dx_ref,
-    din_ref,
-    dout_ref,
+    owners,
     vstage,
     ustage,
     vrecv,
@@ -53,6 +63,7 @@
     irecv,
     send,
     recv,
+    local,
 ):
     h = lax.axis_index("group")
     m = lax.axis_index("mp")
@@ -61,7 +72,7 @@
     blocks = slot_ref.shape[0]
     block_rows = rows // blocks
     shard = rows // mps
-    slots = dev_ref.shape[1]
+    slots = dev_ref.shape[0]
 
     def offset(i, n):
         k = i // 2 + 1
@@ -69,7 +80,8 @@
 
     def to_groups(which, src, dst):
         def step(i, carry):
-            j = lax.rem(h + offset(i, groups), groups)
+            k = groups // 2 - (i + 1) // 2
+            j = lax.rem(h + (i % 2) * (groups - 2 * k) + k, groups)
             pltpu.make_async_remote_copy(
                 src_ref=src(j),
                 dst_ref=dst,
@@ -125,36 +137,78 @@
 
         lax.fori_loop(1, n, greet, 0)
 
-    def stage(j, carry):
+    loads = {
+        which: pltpu.make_async_copy(src, dst, local.at[which])
+        for which, src, dst in (
+            (VIN, vin_hbm, vin_ref),
+            (GATE, gate_hbm, gate_ref),
+            (ROWS, x_hbm, x_ref),
+            (UIN, uin_hbm, uin_ref),
+            (COT, g_hbm, g_ref),
+            (BIAS, bias_hbm, bias_ref),
+        )
+    }
+    for load in loads.values():
+        load.start()
+
+    def stage_panels(panels, staged, received):
+        def stage(j, carry):
+            for s in range(slots):
+                staged[j, s] = panels[dev_ref[s, j]]
+            return carry
+
+        lax.fori_loop(0, groups, stage, 0)
         for s in range(slots):
-            e = dev_ref[j, s]
-            vstage[j, s] = vin_ref[e]
-            ustage[j, s] = uin_ref[e]
-        return carry
-
-    lax.fori_loop(0, groups, stage, 0)
-    for s in range(slots):
-        vrecv[s, part(h, piece), :] = vstage[h, s]
-        urecv[s, part(h, piece), :] = ustage[h, s]
+            received[s, part(h, piece), :] = staged[h, s]
+
+    loads[VIN].wait()
+    stage_panels(vin_ref, vstage, vrecv)
+    pl.semaphore_wait(barrier, groups + mps - 2)
+    to_groups(VPANEL, lambda j: vstage.at[j], vrecv.at[:, part(h, piece), :])
+    loads[UIN].wait()
+    stage_panels(uin_ref, ustage, urecv)
+    to_groups(UPANEL, lambda j: ustage.at[j], urecv.at[:, part(h, piece), :])
 
     slot_of = [slot_ref[b] for b in range(blocks)]
-    gate_row = [gate_ref[dev_ref[h, slot_of[b]]] for b in range(blocks)]
+    expert_of = [dev_ref[slot_of[b], h] for b in range(blocks)]
     alive = [(live_ref[0] > b).astype(F32) for b in range(blocks)]
     which_row = lax.broadcasted_iota(jnp.int32, (8, block_rows), 0)
+
+    loads[GATE].wait()
+    gate_lane = lax.broadcasted_iota(jnp.int32, (8, experts), 1)
+    gate_sub = lax.broadcasted_iota(jnp.int32, (8, experts), 0)
+    picks = jnp.zeros((8, experts), F32)
+    for b in range(blocks):
+        here = (gate_lane == expert_of[b]).astype(F32)
+        picks = jnp.where(gate_sub == b, here, picks)
+    gate_rows = jnp.dot(picks.astype(BF16), gate_ref[...], preferred_element_type=F32)
+    loads[ROWS].wait()
     logits = jnp.zeros((8, block_rows), F32)
     live_rows = jnp.zeros((8, block_rows), F32)
     for b in range(blocks):
-        wide = jnp.broadcast_to(gate_row[b], (8, width)).astype(BF16)
-        scores = lax.dot_general(wide, x_ref[block(b), :], NT, preferred_element_type=F32)
+        scores = lax.dot_general(
+            gate_rows.astype(BF16), x_ref[block(b), :], NT, preferred_element_type=F32
+        )
         logits = jnp.where(which_row == b, scores, logits)
         live_rows = jnp.where(which_row == b, alive[b], live_rows)
     lsend[...] = logits
     lrecv[m] = logits
 
-    pl.semaphore_wait(barrier, groups + mps - 2)
-
-    to_groups(VPANEL, lambda j: vstage.at[j], vrecv.at[:, part(h, piece), :])
     to_mps(LOGIT, lambda j: lsend, lrecv.at[m])
+
+    lane = lax.broadcasted_iota(jnp.int32, (1, groups * slots * piece), 1)
+
+    def encode(j, code):
+        for s in range(slots):
+            code = code + (lane // piece == j * slots + s).astype(jnp.int32) * dev_ref[s, j] * piece
+        return code
+
+    code = lax.fori_loop(0, groups, encode, lane % piece)
+    owners[...] = (
+        (lax.broadcasted_iota(jnp.int32, owners.shape, 0) == code).astype(F32).astype(BF16)
+    )
+    loads[COT].wait()
+    loads[BIAS].wait()
     drain(lrecv.at[pl.ds(0, mps - 1)], recv.at[LOGIT])
     prob = jax.nn.sigmoid(jnp.sum(lrecv[...], axis=0))
     scaled = live_rows * prob
@@ -165,7 +219,6 @@
         ).astype(BF16)
 
     drain(vrecv.at[:, pl.ds(0, width - piece), :], recv.at[VPANEL])
-    to_groups(UPANEL, lambda j: ustage.at[j], urecv.at[:, part(h, piece), :])
     for b in range(blocks):
         rsend[block(b), :] = jnp.dot(
             x_ref[block(b), :], vrecv[slot_of[b]], preferred_element_type=F32
@@ -247,23 +300,30 @@
         total = dpart[block(b), :] + lax.dot_general(
             rgrad[block(b), :], vrecv[slot_of[b]], NT, preferred_element_type=F32
         )
-        total = total + column(gate_back[b : b + 1, :]) * gate_row[b]
+        total = total + column(gate_back[b : b + 1, :]) * gate_rows[b : b + 1, :]
         dx_ref[block(b), :] = total.astype(BF16)
 
-    owners = (
-        lax.broadcasted_iota(jnp.int32, (experts * piece, groups * slots * piece), 0)
-        == code_ref[...]
-    ).astype(F32).astype(BF16)
+    stores = {
+        which: pltpu.make_async_copy(src, dst, local.at[which])
+        for which, src, dst in (
+            (DX_OUT, dx_ref, dx_hbm),
+            (DIN_OUT, din_ref, din_hbm.at[:, 0]),
+            (DOUT_OUT, dout_ref, dout_hbm.at[:, 0]),
+        )
+    }
+    stores[DX_OUT].start()
 
     def owner_sums(received, out):
         flat = received[...].reshape(groups * slots * piece, rank)
-        total = jnp.dot(owners, flat, preferred_element_type=F32)
+        total = jnp.dot(owners[...], flat, preferred_element_type=F32)
         out[...] = total.astype(BF16).reshape(experts, piece, rank)
 
     drain(orecv.at[pl.ds(0, groups - 1)], recv.at[DOUT])
     owner_sums(orecv, dout_ref)
+    stores[DOUT_OUT].start()
     drain(irecv.at[pl.ds(0, groups - 1)], recv.at[DIN])
     owner_sums(irecv, din_ref)
+    stores[DIN_OUT].start()
 
     drain(vstage.at[pl.ds(0, groups - 1)], send.at[VPANEL])
     drain(ustage.at[pl.ds(0, groups - 1)], send.at[UPANEL])
@@ -275,6 +335,22 @@
     drain(brecv.at[pl.ds(0, mps - 1)], send.at[BACK])
     drain(tanh_all.at[pl.ds(0, rows - shard), :], send.at[TANH])
     drain(rgrad.at[pl.ds(0, rows - shard), :], send.at[RGRAD])
+    for store in stores.values():
+        store.wait()
+
+
+def write_out(*refs):
+    sources, targets, held = refs[0:3], refs[3:6], refs[6:9]
+    came, went = refs[9:]
+    loads = [pltpu.make_async_copy(sources[i], held[i], came.at[i]) for i in range(3)]
+    stores = [pltpu.make_async_copy(held[i], targets[i], went.at[i]) for i in range(3)]
+    for load in loads:
+        load.start()
+    for load, store in zip(loads, stores):
+        load.wait()
+        store.start()
+    for store in stores:
+        store.wait()
 
 
 def per_device(
@@ -295,22 +371,28 @@
     rows, width = base_rows.shape
     shard = rows // mps
     lanes = rows // block_slot.shape[0]
-    gates = jnp.transpose(gating_weight_matrix).astype(F32).reshape(experts, 1, width)
-    code = (
-        dev_experts.reshape(groups * slots, 1) * piece + jnp.arange(piece, dtype=jnp.int32)[None, :]
-    ).reshape(1, groups * slots * piece)
-    vmem = pl.BlockSpec(memory_space=pltpu.VMEM)
     smem = pl.BlockSpec(memory_space=pltpu.SMEM)
-    dx, din, dout = pl.pallas_call(
+    hbm = pl.BlockSpec(memory_space=pltpu.HBM)
+    results = pl.pallas_call(
         functools.partial(kernel, groups, mps),
         out_shape=(
             jax.ShapeDtypeStruct((rows, width), BF16),
-            jax.ShapeDtypeStruct((experts, piece, rank), BF16),
-            jax.ShapeDtypeStruct((experts, piece, rank), BF16),
+            jax.ShapeDtypeStruct((experts, 1, piece, rank), BF16),
+            jax.ShapeDtypeStruct((experts, 1, piece, rank), BF16),
         ),
-        in_specs=[smem] * 3 + [vmem] * 7,
-        out_specs=(vmem, vmem, vmem),
+        in_specs=[smem] * 3 + [hbm] * 6,
+        out_specs=(hbm, hbm, hbm),
         scratch_shapes=[
+            pltpu.VMEM((rows, width), BF16),
+            pltpu.VMEM((experts, piece, rank), BF16),
+            pltpu.VMEM((experts, piece, rank), BF16),
+            pltpu.VMEM((rows, width), BF16),
+            pltpu.VMEM((rows, width), BF16),
+            pltpu.VMEM((experts, piece, rank), BF16),
+            pltpu.VMEM((experts, piece, rank), BF16),
+            pltpu.VMEM((experts, width), BF16),
+            pltpu.VMEM((1, width), F32),
+            pltpu.VMEM((experts * piece, groups * slots * piece), BF16),
             pltpu.VMEM((groups, slots, piece, rank), BF16),
             pltpu.VMEM((groups, slots, piece, rank), BF16),
             pltpu.VMEM((slots, width, rank), BF16),
@@ -334,27 +416,31 @@
             pltpu.VMEM((groups, slots, piece, rank), BF16),
             pltpu.SemaphoreType.DMA((10,)),
             pltpu.SemaphoreType.DMA((10,)),
+            pltpu.SemaphoreType.DMA((9,)),
         ],
         compiler_params=pltpu.CompilerParams(
-            collective_id=0, has_side_effects=True, vmem_limit_bytes=40 * 1024 * 1024
+            collective_id=0, has_side_effects=True, vmem_limit_bytes=60 * 1024 * 1024
         ),
     )(
-        dev_experts,
+        jnp.transpose(dev_experts),
         block_slot,
         live_blocks,
-        code,
         base_rows,
         cotangent,
         in_panels.reshape(experts, piece, rank),
         out_panels.reshape(experts, piece, rank),
-        gates,
+        jnp.transpose(gating_weight_matrix),
         cross_bias.reshape(1, width),
     )
-    return (
-        dx,
-        din.reshape(experts, 1, piece, rank),
-        dout.reshape(experts, 1, piece, rank),
-    )
+    return pl.pallas_call(
+        write_out,
+        out_shape=tuple(jax.ShapeDtypeStruct(a.shape, a.dtype) for a in results),
+        in_specs=[hbm] * 3,
+        out_specs=(hbm, hbm, hbm),
+        scratch_shapes=[pltpu.VMEM(a.shape, a.dtype) for a in results]
+        + [pltpu.SemaphoreType.DMA((3,)), pltpu.SemaphoreType.DMA((3,))],
+        compiler_params=pltpu.CompilerParams(vmem_limit_bytes=60 * 1024 * 1024),
+    )(*results)
 
 
 def solution(mesh):

time: 137 us -> 123 us (0.90)
  local copies, waits for them, and re-layouts: 6.94 us -> 0 us
  Pallas kernels: 127 us -> 121 us
  other arithmetic: 1.53 us -> 0 us
    pallas_call x1, Pallas kernels: 127 us -> 119 us  [per_device(): pl.pallas_call(functools.partial(kernel, groups, mps), out_shape=(jax.Sha...]
    unnamed x16 -> x0, local copies, waits for them, and re-layouts: 6.61 us -> none
    pallas_call x0 -> x1, Pallas kernels: none -> 2.05 us  [per_device(): pl.pallas_call(write_out, out_shape=tuple((jax.ShapeDtypeStruct(a.shape,...]
where the time goes in v2:
time: 123 us
  Pallas kernels  121 us (98%)
  between operations  1.29 us (1%)
    pallas_call x1, Pallas kernels, per_device(): pl.pallas_call(functools.partial(kernel, groups, mps), out_shape=(jax.Sha...  119 us

profile of v2, /device:TPU:1, one launch (start us, length us, event | category | flops | bytes accessed | tf_op | source)
XLA Modules:
  0.0 122.7 jit_solution(16709156999564023484)
XLA Ops:
  1.3 119.4 %shard_map.112 = (bf16[512,512]{1,0:T(8,128)(2,1)}, bf16[32,1,16,256]{3,2,1,0:T(8,128)(2,1)}, bf16[32,1,16,256]{3,2,1,0:T(8,128)(2,1)}) custom-call(s32[2,32]{1,0:T(2,128)} %bitcast.9, s32[4]{0:T(128)} %slot_ref.1, s32[1]{0:T(128)S(6)} %copy.12.live_ref, bf16[512,512]{1,0:T(8,128)(2,1)} %x_hbm.1, bf16[512,512]{1,0:T(8,128)(2,1)} %g_hbm.1, ...), custom_call_target="tpu_custom_call" | custom-call | tf_op jit(solution)/shard_map/pallas_call | solution.py:376
  120.7 2.1 %shard_map.113 = (bf16[512,512]{1,0:T(8,128)(2,1)}, bf16[32,1,16,256]{3,2,1,0:T(8,128)(2,1)}, bf16[32,1,16,256]{3,2,1,0:T(8,128)(2,1)}) custom-call(bf16[512,512]{1,0:T(8,128)(2,1)} %get-tuple-element.6.refs_0_, bf16[32,1,16,256]{3,2,1,0:T(8,128)(2,1)} %get-tuple-element.7.refs_1_, bf16[32,1,16,256]{3,2,1,0:T(8,128)(2,1)} %get-tuple-element.8.refs_2_), custom_call_target="tpu_custom_call" | custom-call | tf_op jit(solution)/shard_map/pallas_call | solution.py:435

commit v3 on v2

--- a/solution.py
+++ b/solution.py
@@ -11,7 +11,9 @@
 BF16 = jnp.bfloat16
 NT = (((1,), (1,)), ((), ()))
 TN = (((0,), (0,)), ((), ()))
-LOGIT, VPANEL, UPANEL, RANK, TANH, DOUT, BACK, RGRAD, GSUM, DIN = range(10)
+HALVES = 2
+LOGIT, GSUM, DOUT, DIN = range(4)
+VPANEL, UPANEL, RANK, TANH, BACK, RGRAD = range(4, 4 + 6 * HALVES, HALVES)
 VIN, GATE, ROWS, COT, UIN, BIAS, DX_OUT, DIN_OUT, DOUT_OUT = range(9)
 
 
@@ -42,8 +44,10 @@
     owners,
     vstage,
     ustage,
-    vrecv,
-    urecv,
+    vfirst,
+    vsecond,
+    ufirst,
+    usecond,
     lsend,
     lrecv,
     rsend,
@@ -73,6 +77,8 @@
     block_rows = rows // blocks
     shard = rows // mps
     slots = dev_ref.shape[0]
+    half = rank // HALVES
+    vrecv, urecv = (vfirst, vsecond), (ufirst, usecond)
 
     def offset(i, n):
         k = i // 2 + 1
@@ -154,20 +160,32 @@
     def stage_panels(panels, staged, received):
         def stage(j, carry):
             for s in range(slots):
-                staged[j, s] = panels[dev_ref[s, j]]
+                panel = panels[dev_ref[s, j]]
+                for a in range(HALVES):
+                    staged[a, j, s] = panel[:, a * half : (a + 1) * half]
             return carry
 
         lax.fori_loop(0, groups, stage, 0)
-        for s in range(slots):
-            received[s, part(h, piece), :] = staged[h, s]
+        for a in range(HALVES):
+            for s in range(slots):
+                received[a][s, part(h, piece), :] = staged[a, h, s]
+
+    def send_panels(which, staged, received):
+        for a in range(HALVES):
+            to_groups(
+                which + a, lambda j, a=a: staged.at[a, j], received[a].at[:, part(h, piece), :]
+            )
+
+    def await_panel(which, a, received):
+        drain(received[a].at[:, pl.ds(0, width - piece), :], recv.at[which + a])
 
     loads[VIN].wait()
     stage_panels(vin_ref, vstage, vrecv)
     pl.semaphore_wait(barrier, groups + mps - 2)
-    to_groups(VPANEL, lambda j: vstage.at[j], vrecv.at[:, part(h, piece), :])
+    send_panels(VPANEL, vstage, vrecv)
     loads[UIN].wait()
     stage_panels(uin_ref, ustage, urecv)
-    to_groups(UPANEL, lambda j: ustage.at[j], urecv.at[:, part(h, piece), :])
+    send_panels(UPANEL, ustage, urecv)
 
     slot_of = [slot_ref[b] for b in range(blocks)]
     expert_of = [dev_ref[slot_of[b], h] for b in range(blocks)]
@@ -218,20 +236,42 @@
             gate * x_ref[block(b), :].astype(F32) * g_ref[block(b), :].astype(F32)
         ).astype(BF16)
 
-    drain(vrecv.at[:, pl.ds(0, width - piece), :], recv.at[VPANEL])
-    for b in range(blocks):
-        rsend[block(b), :] = jnp.dot(
-            x_ref[block(b), :], vrecv[slot_of[b]], preferred_element_type=F32
-        ).astype(rsend.dtype)
-    to_mps(RANK, lambda j: rsend.at[part(j, shard), :], rrecv.at[m])
-    rrecv[m] = rsend[part(m, shard), :]
-    drain(rrecv.at[pl.ds(0, mps - 1)], recv.at[RANK])
-    tanh_full = jnp.tanh(jnp.sum(rrecv[...].astype(F32), axis=0))
-    tanh_own[...] = tanh_full
-    tanh_all[part(m, shard), :] = tanh_full.astype(BF16)
-    mine = tanh_all.at[part(m, shard), :]
-    to_mps(TANH, lambda j: mine, mine)
-    drain(tanh_all.at[pl.ds(0, rows - shard), :], recv.at[TANH])
+    def exchange(which, a, left, panels, sent, received):
+        for b in range(blocks):
+            sent[a, block(b), :] = jnp.dot(
+                left[block(b), :], panels[a][slot_of[b]], preferred_element_type=F32
+            )
+        to_mps(which + a, lambda j: sent.at[a, part(j, shard), :], received.at[a, m])
+        received[a, m] = sent[a, part(m, shard), :]
+
+    def total(which, a, received):
+        drain(received.at[a, pl.ds(0, mps - 1)], recv.at[which + a])
+        return jnp.sum(received[a], axis=0)
+
+    def share(which, a, gathered, value):
+        gathered[a, part(m, shard), :] = value.astype(BF16)
+        mine = gathered.at[a, part(m, shard), :]
+        to_mps(which + a, lambda j: mine, mine)
+
+    def await_shared(which, gathered):
+        for a in range(HALVES):
+            drain(gathered.at[a, pl.ds(0, rows - shard), :], recv.at[which + a])
+        return jnp.concatenate([gathered[a] for a in range(HALVES)], axis=1)
+
+    for a in range(HALVES):
+        await_panel(VPANEL, a, vrecv)
+        exchange(RANK, a, x_ref, vrecv, rsend, rrecv)
+        tanh_full = jnp.tanh(total(RANK, a, rrecv))
+        tanh_own[a] = tanh_full
+        share(TANH, a, tanh_all, tanh_full)
+
+    def share_rank_back(a):
+        back_rank = total(BACK, a, brecv)
+        tanh_mine = tanh_own[a]
+        share(RGRAD, a, rgrad, back_rank * (1.0 - tanh_mine * tanh_mine))
+
+    await_panel(UPANEL, 0, urecv)
+    exchange(BACK, 0, gated, urecv, bsend, brecv)
 
     def by_slot(value):
         parts = []
@@ -244,29 +284,29 @@
             parts.append(jnp.concatenate(held, axis=0))
         return parts
 
-    for s, right in enumerate(by_slot(tanh_all[...])):
+    for s, right in enumerate(by_slot(await_shared(TANH, tanh_all))):
         osend[s] = lax.dot_general(gated[...], right, TN, preferred_element_type=F32).astype(
             osend.dtype
         )
     to_groups(DOUT, lambda j: osend.at[:, part(j, piece), :], orecv.at[h])
     orecv[h] = osend[:, part(h, piece), :]
 
-    drain(urecv.at[:, pl.ds(0, width - piece), :], recv.at[UPANEL])
-    for b in range(blocks):
-        bsend[block(b), :] = jnp.dot(
-            gated[block(b), :], urecv[slot_of[b]], preferred_element_type=F32
-        ).astype(bsend.dtype)
-    to_mps(BACK, lambda j: bsend.at[part(j, shard), :], brecv.at[m])
-    brecv[m] = bsend[part(m, shard), :]
+    share_rank_back(0)
+    for a in range(1, HALVES):
+        await_panel(UPANEL, a, urecv)
+        exchange(BACK, a, gated, urecv, bsend, brecv)
+
+    def back_to_width(left, panels, b):
+        return sum(
+            lax.dot_general(
+                left[a, block(b), :], panels[a][slot_of[b]], NT, preferred_element_type=F32
+            )
+            for a in range(HALVES)
+        )
 
     sums = jnp.zeros((8, block_rows), F32)
     for b in range(blocks):
-        cross = (
-            lax.dot_general(
-                tanh_all[block(b), :], urecv[slot_of[b]], NT, preferred_element_type=F32
-            )
-            + bias_ref[...]
-        )
+        cross = back_to_width(tanh_all, urecv, b) + bias_ref[...]
         gate = column(scaled[b : b + 1, :])
         full = g_ref[block(b), :].astype(F32)
         dpart[block(b), :] = full * (1.0 + gate * cross)
@@ -280,14 +320,9 @@
     qrecv[m] = sums
     to_mps(GSUM, lambda j: qsend, qrecv.at[m])
 
-    drain(brecv.at[pl.ds(0, mps - 1)], recv.at[BACK])
-    back_rank = jnp.sum(brecv[...].astype(F32), axis=0)
-    tanh_mine = tanh_own[...]
-    rgrad[part(m, shard), :] = (back_rank * (1.0 - tanh_mine * tanh_mine)).astype(BF16)
-    own = rgrad.at[part(m, shard), :]
-    to_mps(RGRAD, lambda j: own, own)
-    drain(rgrad.at[pl.ds(0, rows - shard), :], recv.at[RGRAD])
-    for s, right in enumerate(by_slot(rgrad[...])):
+    for a in range(1, HALVES):
+        share_rank_back(a)
+    for s, right in enumerate(by_slot(await_shared(RGRAD, rgrad))):
         isend[s] = lax.dot_general(x_ref[...], right, TN, preferred_element_type=F32).astype(
             isend.dtype
         )
@@ -297,11 +332,9 @@
     drain(qrecv.at[pl.ds(0, mps - 1)], recv.at[GSUM])
     gate_back = scaled * (1.0 - prob) * jnp.sum(qrecv[...], axis=0)
     for b in range(blocks):
-        total = dpart[block(b), :] + lax.dot_general(
-            rgrad[block(b), :], vrecv[slot_of[b]], NT, preferred_element_type=F32
-        )
-        total = total + column(gate_back[b : b + 1, :]) * gate_rows[b : b + 1, :]
-        dx_ref[block(b), :] = total.astype(BF16)
+        d_rows = dpart[block(b), :] + back_to_width(rgrad, vrecv, b)
+        d_rows = d_rows + column(gate_back[b : b + 1, :]) * gate_rows[b : b + 1, :]
+        dx_ref[block(b), :] = d_rows.astype(BF16)
 
     stores = {
         which: pltpu.make_async_copy(src, dst, local.at[which])
@@ -325,16 +358,17 @@
     owner_sums(irecv, din_ref)
     stores[DIN_OUT].start()
 
-    drain(vstage.at[pl.ds(0, groups - 1)], send.at[VPANEL])
-    drain(ustage.at[pl.ds(0, groups - 1)], send.at[UPANEL])
+    for a in range(HALVES):
+        drain(vstage.at[a, pl.ds(0, groups - 1)], send.at[VPANEL + a])
+        drain(ustage.at[a, pl.ds(0, groups - 1)], send.at[UPANEL + a])
+        drain(rrecv.at[a, pl.ds(0, mps - 1)], send.at[RANK + a])
+        drain(brecv.at[a, pl.ds(0, mps - 1)], send.at[BACK + a])
+        drain(tanh_all.at[a, pl.ds(0, rows - shard), :], send.at[TANH + a])
+        drain(rgrad.at[a, pl.ds(0, rows - shard), :], send.at[RGRAD + a])
     drain(orecv.at[pl.ds(0, groups - 1)], send.at[DOUT])
     drain(irecv.at[pl.ds(0, groups - 1)], send.at[DIN])
     drain(lrecv.at[pl.ds(0, mps - 1)], send.at[LOGIT])
     drain(qrecv.at[pl.ds(0, mps - 1)], send.at[GSUM])
-    drain(rrecv.at[pl.ds(0, mps - 1)], send.at[RANK])
-    drain(brecv.at[pl.ds(0, mps - 1)], send.at[BACK])
-    drain(tanh_all.at[pl.ds(0, rows - shard), :], send.at[TANH])
-    drain(rgrad.at[pl.ds(0, rows - shard), :], send.at[RGRAD])
     for store in stores.values():
         store.wait()
 
@@ -393,19 +427,21 @@
             pltpu.VMEM((experts, width), BF16),
             pltpu.VMEM((1, width), F32),
             pltpu.VMEM((experts * piece, groups * slots * piece), BF16),
-            pltpu.VMEM((groups, slots, piece, rank), BF16),
-            pltpu.VMEM((groups, slots, piece, rank), BF16),
-            pltpu.VMEM((slots, width, rank), BF16),
-            pltpu.VMEM((slots, width, rank), BF16),
+            pltpu.VMEM((HALVES, groups, slots, piece, rank // HALVES), BF16),
+            pltpu.VMEM((HALVES, groups, slots, piece, rank // HALVES), BF16),
+            pltpu.VMEM((slots, width, rank // HALVES), BF16),
+            pltpu.VMEM((slots, width, rank // HALVES), BF16),
+            pltpu.VMEM((slots, width, rank // HALVES), BF16),
+            pltpu.VMEM((slots, width, rank // HALVES), BF16),
             pltpu.VMEM((8, lanes), F32),
             pltpu.VMEM((mps, 8, lanes), F32),
-            pltpu.VMEM((rows, rank), BF16),
-            pltpu.VMEM((mps, shard, rank), BF16),
-            pltpu.VMEM((rows, rank), BF16),
-            pltpu.VMEM((shard, rank), F32),
-            pltpu.VMEM((rows, rank), BF16),
-            pltpu.VMEM((mps, shard, rank), BF16),
-            pltpu.VMEM((rows, rank), BF16),
+            pltpu.VMEM((HALVES, rows, rank // HALVES), F32),
+            pltpu.VMEM((HALVES, mps, shard, rank // HALVES), F32),
+            pltpu.VMEM((HALVES, rows, rank // HALVES), BF16),
+            pltpu.VMEM((HALVES, shard, rank // HALVES), F32),
+            pltpu.VMEM((HALVES, rows, rank // HALVES), F32),
+            pltpu.VMEM((HALVES, mps, shard, rank // HALVES), F32),
+            pltpu.VMEM((HALVES, rows, rank // HALVES), BF16),
             pltpu.VMEM((8, lanes), F32),
             pltpu.VMEM((mps, 8, lanes), F32),
             pltpu.VMEM((rows, width), BF16),
@@ -414,8 +450,8 @@
             pltpu.VMEM((groups, slots, piece, rank), BF16),
             pltpu.VMEM((slots, width, rank), BF16),
             pltpu.VMEM((groups, slots, piece, rank), BF16),
-            pltpu.SemaphoreType.DMA((10,)),
-            pltpu.SemaphoreType.DMA((10,)),
+            pltpu.SemaphoreType.DMA((4 + 6 * HALVES,)),
+            pltpu.SemaphoreType.DMA((4 + 6 * HALVES,)),
             pltpu.SemaphoreType.DMA((9,)),
         ],
         compiler_params=pltpu.CompilerParams(

time: 123 us -> 123 us (level)
  no operation moved by 1% of the time
where the time goes in v3:
time: 123 us
  Pallas kernels  122 us (99%)
  between operations  1.29 us (1%)
    pallas_call x1, Pallas kernels, per_device(): pl.pallas_call(functools.partial(kernel, groups, mps), out_shape=(jax.Sha...  120 us

profile of v3, /device:TPU:1, one launch (start us, length us, event | category | flops | bytes accessed | tf_op | source)
XLA Modules:
  0.0 122.9 jit_solution(11637542450321900959)
XLA Ops:
  1.3 119.6 %shard_map.112 = (bf16[512,512]{1,0:T(8,128)(2,1)}, bf16[32,1,16,256]{3,2,1,0:T(8,128)(2,1)}, bf16[32,1,16,256]{3,2,1,0:T(8,128)(2,1)}) custom-call(s32[2,32]{1,0:T(2,128)} %bitcast.9, s32[4]{0:T(128)} %slot_ref.1, s32[1]{0:T(128)S(6)} %copy.12.live_ref, bf16[512,512]{1,0:T(8,128)(2,1)} %x_hbm.1, bf16[512,512]{1,0:T(8,128)(2,1)} %g_hbm.1, ...), custom_call_target="tpu_custom_call" | custom-call | tf_op jit(solution)/shard_map/pallas_call | solution.py:410
  120.9 2.1 %shard_map.113 = (bf16[512,512]{1,0:T(8,128)(2,1)}, bf16[32,1,16,256]{3,2,1,0:T(8,128)(2,1)}, bf16[32,1,16,256]{3,2,1,0:T(8,128)(2,1)}) custom-call(bf16[512,512]{1,0:T(8,128)(2,1)} %get-tuple-element.6.refs_0_, bf16[32,1,16,256]{3,2,1,0:T(8,128)(2,1)} %get-tuple-element.7.refs_1_, bf16[32,1,16,256]{3,2,1,0:T(8,128)(2,1)} %get-tuple-element.8.refs_2_), custom_call_target="tpu_custom_call" | custom-call | tf_op jit(solution)/shard_map/pallas_call | solution.py:471
